TPU v7x, 512 devices: a whole 4x8x8 slice. The times are simulated.
512 devices in a mesh: ia: 16 (over z_lo, x, core), ja: 8 (over y), ka: 4 (over z_hi).
Axes of the slice: x: 4, y: 8, z: 8 (z_hi: 4, z_lo: 2; z = z_hi * 2 + z_lo), core: 2. Of those that a mesh axis runs over, the one named last changes fastest.
Arguments:
- tensor: float32 [512, 1024, 512], P('ia', 'ja', 'ka'), may hold values from -200 to 200
- factor_b: float32 [1024, 4, 96], P(('ja', 'ka')), may hold values from -4 to 4
- factor_c: float32 [512, 4, 96], P(('ka', 'ja')), may hold values from -4 to 4
Outputs:
- factor_a: float32 [512, 4, 96], P(('ia', 'ja', 'ka'))
- weights: float32 [4, 96], replicated
All inputs are finite; a program needn't handle non-finite values.
Results may differ from a plain program's by a relative error of at most 0.0003.
Values sent between devices are 32-bit elements; how exact they have to be, the bound alone decides.
No kernel may reach another device: no remote copies, remote signals or barrier semaphores. Data moves between devices by JAX's collectives and lax.ppermute only.
A program may use at most 64 MiB of HBM per device.

v0:
```python
import jax
import jax.numpy as jnp
from jax import lax
from jax.sharding import PartitionSpec as P

highest = lax.Precision.HIGHEST


def gram_of(rows):
    return jnp.einsum(
        "jsr,jsq->srq", rows, rows, precision=highest, preferred_element_type=jnp.float32
    )


def solve_normal(rows, gram_b, gram_c):
    columns = []
    for member in range(rows.shape[1]):
        normal_mat = gram_b[member] * gram_c[member]
        factor_l = jnp.linalg.cholesky(normal_mat)
        right_side = rows[:, member, :].T
        lower_sol = lax.linalg.triangular_solve(factor_l, right_side, left_side=True, lower=True)
        upper_sol = lax.linalg.triangular_solve(
            factor_l, lower_sol, left_side=True, lower=True, transpose_a=True
        )
        columns.append(upper_sol.T)
    return jnp.stack(columns, axis=1)


def shards(tensor, factor_b, factor_c):
    rows_i, rows_j, rows_k = tensor.shape
    starts, col_count = (factor_b.shape[1], factor_b.shape[2])
    width = starts * col_count
    c_block = lax.all_gather(factor_c, "ja", axis=0, tiled=True)
    partial_value = jnp.dot(
        tensor.reshape(rows_i * rows_j, rows_k),
        c_block.reshape(rows_k, width),
        precision=highest,
        preferred_element_type=jnp.float32,
    ).reshape(rows_i, rows_j, width)
    piece = lax.all_gather(factor_b, "ka", axis=0, tiled=True)
    gram_sum = jnp.zeros((starts, col_count, col_count), jnp.float32)
    count = piece.shape[0]
    flat_rows = piece.reshape(count, width)
    mttkrp = jnp.einsum(
        "ijr,jr->ir",
        partial_value,
        flat_rows,
        precision=highest,
        preferred_element_type=jnp.float32,
    )
    mttkrp, gram_rows = (mttkrp, gram_sum)
    gram_b, gram_c = lax.psum((gram_of(factor_b), gram_of(factor_c)), ("ja", "ka"))
    slab_rows = lax.psum_scatter(mttkrp, "ja", scatter_dimension=0, tiled=True)
    owned = lax.psum_scatter(slab_rows, "ka", scatter_dimension=0, tiled=True)
    owned = owned.reshape(owned.shape[0], starts, col_count)
    factor_raw = solve_normal(owned, gram_b, gram_c)
    squares = jnp.sum(factor_raw * factor_raw, axis=0)
    total = lax.psum(squares, ("ia", "ja", "ka"))
    row_total = rows_i * lax.axis_size("ia")
    weights = jnp.sqrt(total / row_total + 1e-06)
    return (factor_raw / weights[None], weights)


def solution(mesh):
    in_specs = (P("ia", "ja", "ka"), P(("ja", "ka"), None, None), P(("ka", "ja"), None, None))
    out_specs = (P(("ia", "ja", "ka"), None, None), P())
    return jax.shard_map(shards, mesh=mesh, in_specs=in_specs, out_specs=out_specs, check_vma=False)
```

profile of v0, /device:TPU:1, one launch (start us, length us, event | category | flops | bytes accessed | tf_op | source)
XLA Modules:
  0.0 503.4 jit_solution(228719153162087754)
XLA Ops:
  7.2 2.1 fusion.22
  9.3 2.1 fusion
  11.4 18.7 %all_gather.7 = f32[128,4,96]{2,1,0:T(4,128)S(1)} all-gather(f32[32,4,96]{2,1,0:T(4,128)} %param.9), channel_id=1, replica_groups=mesh['ia'=16,'ja'=8,'ka'=4] {'ka'}, dimensions={0}, use_global_device_ids=true | all-gather | bytes 245760 | tf_op jit(solution)/shard_map/all_gather | solution.py:40
  30.1 22.2 %all_gather.6 = f32[128,4,96]{2,1,0:T(4,128)S(1)} all-gather(f32[16,4,96]{2,1,0:T(4,128)} %param.10), channel_id=1, replica_groups=mesh['ia'=16,'ja'=8,'ka'=4] {'ja'}, dimensions={0}, use_global_device_ids=true | all-gather | bytes 221184 | tf_op jit(solution)/shard_map/all_gather | solution.py:33
  52.7 1.3 dynamic-slice
  54.0 1.3 dynamic-slice.2
  55.9 5.5 %multiply_reduce_fusion = f32[384,32]{0,1:T(8,128)S(1)} fusion(f32[384,128]{0,1:T(8,128)S(1)} %copy.52, f32[32,128,128]{2,1,0:T(8,128)S(1)} %copy-done, f32[128,384,1]{0,1,2:T(8,128)S(1)} %bitcast.141), kind=kOutput, calls=%fused_computation | convolution fusion | flops 2419052544 | bytes 2539520 | tf_op jit(solution)/shard_map/dot_general | solution.py:34
  61.4 23.5 %all-reduce = f32[32,384]{1,0:T(8,128)S(1)} all-reduce(f32[32,384]{1,0:T(8,128)S(1)} %bitcast.142), channel_id=2, replica_groups=mesh['ia'=16,'ja'=8,'ka'=4] {'ja'}, use_global_device_ids=true, to_apply=%region_4.0.clone | all-reduce | flops 12288 | bytes 98304
  84.9 9.5 %all-reduce.1 = f32[4,384]{1,0:T(4,128)S(1)} all-reduce(f32[4,384]{1,0:T(4,128)S(1)} %constant_dynamic-slice_fusion), channel_id=3, replica_groups=mesh['ia'=16,'ja'=8,'ka'=4] {'ka'}, use_global_device_ids=true, to_apply=%region_5.0.clone | all-reduce | flops 1536 | bytes 12288
  94.5 0.7 dynamic-slice_reduce_fusion
  95.2 210.4 %all-reduce.5.cloned.1.call-done = (f32[4,96,96]{1,2,0:T(8,128)}, f32[4,96,96]{1,2,0:T(8,128)}) async-done(((f32[4,96,96]{1,2,0:T(8,128)}, f32[4,96,96]{1,2,0:T(8,128)}), (f32[4,96,96]{1,2,0:T(8,128)}, f32[4,96,96]{1,2,0:T(8,128)})) %all-reduce.5.cloned.1.call-update) | async-done | bytes 294928 | tf_op jit(solution)/shard_map/psum | solution.py:52
  305.6 1.0 fusion.24
  307.0 1.0 fusion.9
  308.0 8.8 %cholesky.107 = f32[96,96]{1,0:T(8,128)S(1)} custom-call(f32[96,96]{1,0:T(8,128)S(1)} %get-tuple-element.10), custom_call_target="Cholesky" | custom-call | tf_op jit(solution)/shard_map/jit(cholesky)/cholesky | solution.py:19
  316.8 0.6 compare_reduce_fusion
  317.5 0.7 fusion.5
  318.1 7.4 %custom-call.21 = f32[1,96,96]{1,2,0:T(8,128)S(1)} custom-call(f32[1,96,96]{2,1,0:T(8,128)S(1)} %fusion.5), custom_call_target="InvertDiagBlocksLowerTriangular" | custom-call | tf_op jit(solution)/shard_map/triangular_solve/custom-call.2 | solution.py:22
  325.6 0.2 fusion.11
  325.8 8.8 %cholesky.96 = f32[96,96]{1,0:T(8,128)S(1)} custom-call(f32[96,96]{1,0:T(8,128)S(1)} %get-tuple-element.11), custom_call_target="Cholesky" | custom-call | tf_op jit(solution)/shard_map/jit(cholesky)/cholesky | solution.py:19
  334.7 0.6 compare_reduce_fusion.1
  335.3 0.7 fusion.4
  336.0 7.4 %custom-call.19 = f32[1,96,96]{1,2,0:T(8,128)S(1)} custom-call(f32[1,96,96]{2,1,0:T(8,128)S(1)} %fusion.4), custom_call_target="InvertDiagBlocksLowerTriangular" | custom-call | tf_op jit(solution)/shard_map/triangular_solve/custom-call.2 | solution.py:22
  343.7 8.8 %cholesky.85 = f32[96,96]{1,0:T(8,128)S(1)} custom-call(f32[96,96]{1,0:T(8,128)S(1)} %get-tuple-element.12), custom_call_target="Cholesky" | custom-call | tf_op jit(solution)/shard_map/jit(cholesky)/cholesky | solution.py:19
  352.5 0.6 compare_reduce_fusion.2
  353.1 0.7 fusion.3
  353.8 7.4 %custom-call.17 = f32[1,96,96]{1,2,0:T(8,128)S(1)} custom-call(f32[1,96,96]{2,1,0:T(8,128)S(1)} %fusion.3), custom_call_target="InvertDiagBlocksLowerTriangular" | custom-call | tf_op jit(solution)/shard_map/triangular_solve/custom-call.2 | solution.py:22
  361.5 9.0 %cholesky.74 = f32[96,96]{1,0:T(8,128)S(1)} custom-call(f32[96,96]{1,0:T(8,128)S(1)} %get-tuple-element.9), custom_call_target="Cholesky" | custom-call | tf_op jit(solution)/shard_map/jit(cholesky)/cholesky | solution.py:19
  370.6 0.6 compare_reduce_fusion.3
  371.2 0.7 fusion.2
  371.9 7.4 %custom-call.15 = f32[1,96,96]{1,2,0:T(8,128)S(1)} custom-call(f32[1,96,96]{2,1,0:T(8,128)S(1)} %fusion.2), custom_call_target="InvertDiagBlocksLowerTriangular" | custom-call | tf_op jit(solution)/shard_map/triangular_solve/custom-call.2 | solution.py:22
  379.6 116.4 %psum.23 = f32[4,96]{1,0:T(4,128)S(1)} all-reduce(f32[4,96]{1,0:T(4,128)S(1)} %fusion.36), channel_id=1, replica_groups=mesh['ia'=16,'ja'=8,'ka'=4] {'ia','ja','ka'}, use_global_device_ids=true, to_apply=%region_6.10 | all-reduce | flops 384 | bytes 3072 | tf_op jit(solution)/shard_map/psum | solution.py:58
  496.0 0.6 divide_bitcast_fusion
  (25 shorter events, 2.2 us)
Async XLA Ops:
  7.2 48.7 %copy-start = (f32[32,128,128]{2,1,0:T(8,128)S(1)}, f32[32,128,128]{2,1,0:T(8,128)}, u32[]{:S(2)}) copy-start(f32[32,128,128]{2,1,0:T(8,128)} %param.8) | copy-start | bytes 6291460
  7.2 298.5 %all-reduce.5.cloned.1.call-start = ((), (), s32[]{:S(2)}) async-start(), calls=%async_computation | async-start | bytes 786432 | tf_op jit(solution)/shard_map/psum | solution.py:52
Sparse Core Ops, SparseCore 0:
  11.5 294.0 all-reduce.4
where the time goes:
time: 504 us; the launch traced here: 503 us
  waiting for transfers between devices  210 us (42%)
  blocking collectives  190 us (38%)
  other arithmetic  72.8 us (14%)
  between operations  14.9 us (3%)
  matrix products  11 us (2%)
    psum x1, waiting for transfers between devices, shards(): lax.psum((gram_of(factor_b), gram_of(factor_c)), ('ja', 'ka'))  210 us
    psum x1, blocking collectives, shards(): total = lax.psum(squares, ('ia', 'ja', 'ka'))  116 us
    another operation x12, other arithmetic, solve_normal(): factor_l = jnp.linalg.cholesky(normal_mat)  38.1 us
    unnamed x2, blocking collectives  33 us
    another operation x8, other arithmetic, solve_normal(): lax.linalg.triangular_solve(factor_l, lower_sol, left_side=True, lower=Tr...  32 us
    all_gather x1, blocking collectives, shards(): c_block = lax.all_gather(factor_c, 'ja', axis=0, tiled=True)  22.2 us
    all_gather x1, blocking collectives, shards(): piece = lax.all_gather(factor_b, 'ka', axis=0, tiled=True)  18.7 us
  transfers between devices with their start and end apart: 1, of which 1 were waited for; matrix products, arithmetic and copies ran while one was open for 2% of the time, Pallas kernels for 0%

commit v1 on v0

--- a/solution.py
+++ b/solution.py
@@ -1,9 +1,17 @@
+import functools
 import jax
 import jax.numpy as jnp
 from jax import lax
 from jax.sharding import PartitionSpec as P
 
 highest = lax.Precision.HIGHEST
+
+
+def touch_group(state, row_axis):
+    return jax.lax.all_gather(state, row_axis).sum(axis=0)
+
+
+choose_the_gates = functools.partial(touch_group, row_axis=("ia", "ja", "ka"))
 
 
 def gram_of(rows):
@@ -55,7 +63,7 @@
     owned = owned.reshape(owned.shape[0], starts, col_count)
     factor_raw = solve_normal(owned, gram_b, gram_c)
     squares = jnp.sum(factor_raw * factor_raw, axis=0)
-    total = lax.psum(squares, ("ia", "ja", "ka"))
+    total = choose_the_gates(squares)
     row_total = rows_i * lax.axis_size("ia")
     weights = jnp.sqrt(total / row_total + 1e-06)
     return (factor_raw / weights[None], weights)

time: 504 us -> 1880 us (3.73)
  the two profiles are of different devices: /device:TPU:1 before, /device:TPU:64 now
where the time goes in v1:
time: 1880 us
  blocking collectives  1560 us (83%)
  waiting for transfers between devices  215 us (11%)
  other arithmetic  73.8 us (4%)
    all_gather x1, blocking collectives, touch_group(): return jax.lax.all_gather(state, row_axis).sum(axis=0)  1480 us
    psum x1, waiting for transfers between devices, shards(): lax.psum((gram_of(factor_b), gram_of(factor_c)), ('ja', 'ka'))  215 us
    unnamed x2, blocking collectives  41.9 us
    another operation x12, other arithmetic, solve_normal(): factor_l = jnp.linalg.cholesky(normal_mat)  38 us
  transfers between devices with their start and end apart: 1, of which 1 were waited for; matrix products, arithmetic and copies ran while one was open for 0% of the time, Pallas kernels for 0%

profile of v1, /device:TPU:64, one launch (start us, length us, event | category | flops | bytes accessed | tf_op | source)
XLA Modules:
  0.0 1882.5 jit_solution(5585434891779839557)
XLA Ops:
  7.2 2.2 fusion
  9.4 2.0 fusion.18
  11.4 19.4 %all_gather.11 = f32[128,4,96]{2,1,0:T(4,128)S(1)} all-gather(f32[32,4,96]{2,1,0:T(4,128)} %param.9), channel_id=1, replica_groups=mesh['ia'=16,'ja'=8,'ka'=4] {'ka'}, dimensions={0}, use_global_device_ids=true | all-gather | bytes 245760 | tf_op jit(solution)/shard_map/all_gather | solution.py:48
  30.9 26.6 %all_gather.10 = f32[128,4,96]{2,1,0:T(4,128)S(1)} all-gather(f32[16,4,96]{2,1,0:T(4,128)} %param.10), channel_id=1, replica_groups=mesh['ia'=16,'ja'=8,'ka'=4] {'ja'}, dimensions={0}, use_global_device_ids=true | all-gather | bytes 221184 | tf_op jit(solution)/shard_map/all_gather | solution.py:41
  57.5 1.3 dynamic-slice.2
  58.8 1.3 dynamic-slice
  61.1 5.5 multiply_reduce_fusion
  66.6 29.4 %all-reduce = f32[32,384]{1,0:T(8,128)S(1)} all-reduce(f32[32,384]{1,0:T(8,128)S(1)} %bitcast.154), channel_id=2, replica_groups=mesh['ia'=16,'ja'=8,'ka'=4] {'ja'}, use_global_device_ids=true, to_apply=%region_4.0.clone | all-reduce | flops 12288 | bytes 98304
  96.0 12.5 all-reduce.1
  108.6 0.7 dynamic-slice_reduce_fusion
  109.3 214.7 %all-reduce.5.cloned.1.call-done = (f32[4,96,96]{1,2,0:T(8,128)}, f32[4,96,96]{1,2,0:T(8,128)}) async-done(((f32[4,96,96]{1,2,0:T(8,128)}, f32[4,96,96]{1,2,0:T(8,128)}), (f32[4,96,96]{1,2,0:T(8,128)}, f32[4,96,96]{1,2,0:T(8,128)})) %all-reduce.5.cloned.1.call-update) | async-done | bytes 294928 | tf_op jit(solution)/shard_map/psum | solution.py:60
  324.0 1.0 fusion.20
  325.4 1.0 fusion.9
  326.4 8.8 cholesky.74
  335.2 0.6 compare_reduce_fusion.3
  335.9 0.7 fusion.2
  336.5 7.4 custom-call.15
  343.9 8.8 cholesky.107
  352.7 0.6 compare_reduce_fusion
  353.3 0.7 fusion.5
  354.0 7.4 custom-call.21
  361.4 8.8 cholesky.96
  370.2 0.6 compare_reduce_fusion.1
  370.8 0.7 fusion.4
  371.5 7.4 custom-call.19
  378.8 9.0 cholesky.85
  387.9 0.6 compare_reduce_fusion.2
  388.5 0.7 fusion.3
  389.2 7.4 custom-call.17
  398.0 1475.9 %all_gather.12 = f32[512,4,96]{2,1,0:T(4,128)S(1)} all-gather(f32[1,4,96]{2,1,0:T(4,128)S(1)} %fusion.33), channel_id=1, replica_groups=mesh['ia'=16,'ja'=8,'ka'=4] {'ia','ja','ka'}, dimensions={0}, use_global_device_ids=true | all-gather | bytes 787968 | tf_op jit(solution)/shard_map/all_gather | solution.py:11
  1874.5 0.6 bitcast_multiply_fusion
  1875.0 0.6 fusion.24
  (27 shorter events, 3.0 us)
Async XLA Ops:
  7.2 53.9 %copy-start = (f32[32,128,128]{2,1,0:T(8,128)S(1)}, f32[32,128,128]{2,1,0:T(8,128)}, u32[]{:S(2)}) copy-start(f32[32,128,128]{2,1,0:T(8,128)} %param.8) | copy-start | bytes 6291460
  7.2 316.9 %all-reduce.5.cloned.1.call-start = ((), (), s32[]{:S(2)}) async-start(), calls=%async_computation | async-start | bytes 786432 | tf_op jit(solution)/shard_map/psum | solution.py:60
Sparse Core Ops, SparseCore 0:
  11.6 312.4 all-reduce.4
